TPU v7x, 256 devices: a whole 4x4x8 slice. The times are simulated.
256 devices in a mesh: dp: 32 (over x, z), seq: 8 (over y, core).
Axes of the slice: x: 4, y: 4, z: 8, core: 2. Of those that a mesh axis runs over, the one named last changes fastest.
Arguments:
- pixels: bfloat16 [32768, 1176], P(('dp', 'seq')), may hold values from -6 to 6
- patch_weight: bfloat16 [1176, 1280], replicated, may hold values from -0.1875 to 0.1875
- ln_gain: float32 [1280], replicated, may hold values from 0.1 to 1.9
- ln_bias: float32 [1280], replicated, may hold values from -1.5 to 1.5
- qkv_weight: bfloat16 [1280, 3840], P('dp'), may hold values from -4 to 4
- qkv_bias: float32 [3840], replicated, may hold values from -2.5 to 2.5
- out_weight: bfloat16 [1280, 1280], P('dp'), may hold values from -0.15625 to 0.15625
- out_bias: float32 [1280], replicated, may hold values from -1.5 to 1.5
- offsets: int32 [32, 3], P('dp'), may hold values from 0 to 854, as said below
- widths: int32 [32, 3], P('dp'), may hold values from 16 to 64
Outputs:
- encoded: bfloat16 [32768, 1280], P(('dp', 'seq'))
Inputs may be any that keep to these rules, and one draw needn't show every extreme that they name: In every group the first offset is 0 and offsets rise; every image holds 170 or more tokens and the last image ends at position 1024; in some group the last image holds exactly 170 tokens.
All inputs are finite; a program needn't handle non-finite values.
Results may differ from a plain program's by a relative error of at most 0.012.
Values may be sent and summed in bfloat16 or wider, within the bound.
No kernel may reach another device: no remote copies, remote signals or barrier semaphores. Data moves between devices by JAX's collectives and lax.ppermute only.
A program may use at most 64 MiB of HBM per device.

v0:
```python
import jax
import jax.numpy as jnp
from jax import lax
from jax.sharding import PartitionSpec as P

HEADS = 16
HDIM = 80


def image_lookup(positions, starts):
    return jnp.sum((positions[:, None] >= starts[None, :]).astype(jnp.int32), axis=1) - 1


def rotation_tables(positions, starts, image_widths, head_size):
    image_index = image_lookup(positions, starts)
    onehot = (image_index[:, None] == jnp.arange(starts.shape[0], dtype=jnp.int32)[None, :]).astype(
        jnp.int32
    )
    first_position = jnp.sum(onehot * starts[None, :], axis=1)
    across = jnp.sum(onehot * image_widths[None, :], axis=1)
    within = positions - first_position
    row_index = within // across
    column_index = within - row_index * across
    quarter = head_size // 4
    inverse = 1.0 / 10000.0 ** (jnp.arange(quarter, dtype=jnp.float32) * 2.0 / (head_size // 2))
    angles = jnp.concatenate(
        [
            row_index.astype(jnp.float32)[:, None] * inverse[None, :],
            column_index.astype(jnp.float32)[:, None] * inverse[None, :],
        ],
        axis=1,
    )
    angles = jnp.concatenate([angles, angles], axis=1)
    return (jnp.cos(angles), jnp.sin(angles), image_index)


def rotate_heads(values, cosine, sine_table, head_size):
    half_size = head_size // 2
    turned = jnp.concatenate([-values[..., half_size:], values[..., :half_size]], axis=-1)
    return values * cosine[:, None, :] + turned * sine_table[:, None, :]


def layer_norm(embedded, ln_gain, ln_bias):
    values = embedded.astype(jnp.float32)
    center = values - jnp.mean(values, axis=-1, keepdims=True)
    variance = jnp.mean(center * center, axis=-1, keepdims=True)
    return (center * lax.rsqrt(variance + 1e-06) * ln_gain + ln_bias).astype(jnp.bfloat16)


def block_length(count):
    length = min(count, 512)
    while count % length:
        length -= 1
    return length


def attend_block(state, queries3, key_block, value_block, query_image, key_image, score_scale):
    running_max, running_total, accum = state
    count = key_block.shape[0]
    scores = (
        jnp.einsum(
            "qhd,khd->hqk",
            queries3,
            key_block.reshape(count, HEADS, HDIM),
            preferred_element_type=jnp.float32,
        )
        * score_scale
    )
    allowed = (query_image[:, None] == key_image[None, :])[None]
    scores = jnp.where(allowed, scores, -1e30)
    new_max = jnp.maximum(running_max, jnp.max(scores, axis=-1))
    weights = jnp.where(allowed, jnp.exp(scores - new_max[..., None]), 0.0)
    factor = jnp.exp(running_max - new_max)
    running_total = running_total * factor + jnp.sum(weights, axis=-1)
    part_sum = jnp.einsum(
        "hqk,khd->qhd",
        weights.astype(jnp.bfloat16),
        value_block.reshape(count, HEADS, HDIM),
        preferred_element_type=jnp.float32,
    )
    accum = accum * factor.T[:, :, None] + part_sum
    return (new_max, running_total, accum)


def per_device(
    pixels,
    patch_weight,
    ln_gain,
    ln_bias,
    qkv_weight,
    qkv_bias,
    out_weight,
    out_bias,
    offsets,
    widths,
):
    local_pixels = lax.all_to_all(pixels, "dp", split_axis=0, concat_axis=0, tiled=True)
    tok_rows = local_pixels.shape[0]
    dmodel = patch_weight.shape[1]
    score_scale = HDIM ** (-0.5)
    embedded = jnp.dot(local_pixels, patch_weight, preferred_element_type=jnp.float32).astype(
        jnp.bfloat16
    )
    normed = layer_norm(embedded, ln_gain, ln_bias)
    columns = normed
    projected = (
        jnp.dot(
            columns,
            lax.all_gather(qkv_weight, "dp", axis=0, tiled=True),
            preferred_element_type=jnp.float32,
        )
        + qkv_bias
    )
    starts = offsets[0]
    image_widths = widths[0]
    positions = lax.axis_index("seq") * tok_rows + jnp.arange(tok_rows, dtype=jnp.int32)
    cosine, sine_table, query_image = rotation_tables(positions, starts, image_widths, HDIM)
    queries = (
        rotate_heads(projected[:, :dmodel].reshape(tok_rows, HEADS, HDIM), cosine, sine_table, HDIM)
        .reshape(tok_rows, dmodel)
        .astype(jnp.bfloat16)
    )
    key_rows = (
        rotate_heads(
            projected[:, dmodel : 2 * dmodel].reshape(tok_rows, HEADS, HDIM),
            cosine,
            sine_table,
            HDIM,
        )
        .reshape(tok_rows, dmodel)
        .astype(jnp.bfloat16)
    )
    values = projected[:, 2 * dmodel :].astype(jnp.bfloat16)
    queries3 = queries.reshape(tok_rows, HEADS, HDIM)
    initial = (
        jnp.full((HEADS, tok_rows), -1e30, jnp.float32),
        jnp.zeros((HEADS, tok_rows), jnp.float32),
        jnp.zeros((tok_rows, HEADS, HDIM), jnp.float32),
    )
    piece_keys = lax.all_gather(key_rows, "seq", axis=0, tiled=True)
    piece_values = lax.all_gather(values, "seq", axis=0, tiled=True)
    count = piece_keys.shape[0]
    length = block_length(count)

    def one_block(block_index, inner):
        first_row = block_index * length
        key_block = lax.dynamic_slice_in_dim(piece_keys, first_row, length, 0)
        value_block = lax.dynamic_slice_in_dim(piece_values, first_row, length, 0)
        key_image = image_lookup(first_row + jnp.arange(length, dtype=jnp.int32), starts)
        return attend_block(
            inner, queries3, key_block, value_block, query_image, key_image, score_scale
        )

    final_state = lax.fori_loop(0, count // length, one_block, initial)
    attended = (
        (final_state[2] / final_state[1].T[:, :, None])
        .reshape(tok_rows, dmodel)
        .astype(jnp.bfloat16)
    )
    columns = attended
    mixed = jnp.dot(
        columns,
        lax.all_gather(out_weight, "dp", axis=0, tiled=True),
        preferred_element_type=jnp.float32,
    )
    return (embedded.astype(jnp.float32) + mixed + out_bias).astype(jnp.bfloat16)


def solution(mesh):
    in_specs = (
        P(("dp", "seq"), None),
        P(),
        P(),
        P(),
        P("dp", None),
        P(),
        P("dp", None),
        P(),
        P("dp", None),
        P("dp", None),
    )
    out_specs = P(("dp", "seq"), None)
    return jax.shard_map(
        per_device, mesh=mesh, in_specs=in_specs, out_specs=out_specs, check_vma=False
    )
```

profile of v0, /device:TPU:8, one launch (start us, length us, event | category | flops | bytes accessed | tf_op | source)
XLA Modules:
  0.0 290.6 jit_solution(15201041775588603741)
XLA Ops:
  6.5 0.7 all-gather.5.cloned.1.call-update
  7.3 1.3 copy.27
  8.6 0.8 all_to_all.8
  9.4 11.4 %all-to-all-start = ((bf16[32,4,1176]{2,1,0:T(4,128)(2,1)}), bf16[32,4,1176]{2,1,0:T(4,128)(2,1)}, u32[]{:S(2)}, u32[]{:S(2)}) async-start(bf16[32,4,1176]{2,1,0:T(4,128)(2,1)} %all_to_all.8), calls=%async_computation | async-start | bytes 655360 | tf_op jit(solution)/shard_map/all_to_all | solution.py:97
  20.9 0.7 convert_reduce_fusion.1
  21.6 0.8 select_reduce_fusion.1
  22.6 0.2 fusion.25
  22.8 0.9 mul.198
  23.7 2.2 copy.28
  25.9 8.5 %all-to-all-done = bf16[32,4,1176]{2,1,0:T(4,128)(2,1)} async-done(((bf16[32,4,1176]{2,1,0:T(4,128)(2,1)}), bf16[32,4,1176]{2,1,0:T(4,128)(2,1)}, u32[]{:S(2)}, u32[]{:S(2)}) %all-to-all-start) | async-done | bytes 301088 | tf_op jit(solution)/shard_map/all_to_all | solution.py:97
  34.4 1.1 all_to_all.10
  35.5 0.7 fusion.28
  36.2 0.8 copy-done.2
  37.1 0.2 multiply_reduce_fusion
  37.3 81.0 %all-gather.5.cloned.1.call-done = bf16[1280,3840]{1,0:T(8,128)(2,1)} async-done(((bf16[40,3840]{1,0:T(8,128)(2,1)}), bf16[1280,3840]{1,0:T(8,128)(2,1)}) %all-gather.5.cloned.1.call-update) | async-done | bytes 9830416 | tf_op jit(solution)/shard_map/all_gather | solution.py:109
  118.3 5.5 %convolution_add_fusion = f32[128,3840]{1,0:T(8,128)S(1)} fusion(bf16[1280,3840]{1,0:T(8,128)(2,1)} %all-gather.5.cloned.1.call-done, f32[3840]{0:T(1024)S(1)} %copy-done.7, f32[128,1280]{1,0:T(8,128)} %copy-done.2, f32[1280]{0:T(1024)S(1)} %copy-done.4, f32[1280]{0:T(1024)S(1)} %copy-done.5, f32[128]{0:T(128)S(1)} %add_rsqrt_fusion, ...), kind=kOutput, calls=%fused_computation.24 | convolution fusion | flops 1259601920 | bytes 12478464 | tf_op jit(solution)/shard_map/dot_general | solution.py:107
  123.8 1.3 copy-done.3
  125.1 1.1 fusion.27
  126.3 2.1 copy.29
  128.4 2.2 copy.32
  130.6 1.4 slice_negate_fusion
  131.9 1.2 maximum_multiply_fusion.1
  133.1 2.2 copy.30
  135.2 2.2 copy.33
  137.4 2.9 add_convert_fusion
  140.4 1.8 slice.41
  142.3 0.5 all-gather.11.cloned.1.call-update
  142.8 1.2 copy.34
  144.0 21.3 %all-gather.7.cloned.1.call-done = bf16[1024,1280]{1,0:T(8,128)(2,1)} async-done(((bf16[128,1280]{1,0:T(8,128)(2,1)}), bf16[1024,1280]{1,0:T(8,128)(2,1)}) %all-gather.7.cloned.1.call-update) | async-done | bytes 2621456 | tf_op jit(solution)/shard_map/all_gather | solution.py:140
  165.3 31.1 %all-gather.9.cloned.1.call-done = bf16[1024,1280]{1,0:T(8,128)(2,1)} async-done(((bf16[128,1280]{1,0:T(8,128)(2,1)}), bf16[1024,1280]{1,0:T(8,128)(2,1)}) %all-gather.9.cloned.1.call-update) | async-done | bytes 2621456 | tf_op jit(solution)/shard_map/all_gather | solution.py:141
  196.5 37.7 %while.20 = (s32[]{:T(128)}, f32[16,128]{1,0:T(8,128)S(1)}, f32[16,128]{1,0:T(8,128)S(1)}, f32[128,16,80]{0,2,1:T(8,128)}, s32[128]{0:T(128)S(1)}, /*index=5*/s3...) while((s32[]{:T(128)}, f32[16,128]{1,0:T(8,128)S(1)}, ...), condition=%wide.region_9.10_spmd.clone, body=%wide.region_5.9_spmd.clone.sunk | while | flops 349750272 | bytes 44511972 | solution.py:154
  196.5 3.5 %constant_dynamic-slice_fusion.3 = (bf16[512,1280]{1,0:T(8,128)(2,1)}, bf16[512,1280]{1,0:T(8,128)(2,1)}) fusion(bf16[1024,1280]{1,0:T(8,128)(2,1)} %get-tuple-element.432, s32[]{:T(128)S(6)} %select_n.85, bf16[1024,1280]{1,0:T(8,128)(2,1)} %get-tuple-element.430), kind=kLoop, calls=%fused_computation.19.clone.1 | loop fusion | bytes 5242884 | tf_op jit(solution)/shard_map/while/body/eval_jaxpr/dynamic_slice | solution.py:148
  199.9 2.4 copy.42
  202.5 0.1 broadcast_compare_fusion.2
  202.6 4.3 %fusion.50 = (f32[16,128]{1,0:T(8,128)S(1)}, f32[16,512,128]{2,1,0:T(8,128)}) fusion(pred[128,512]{0,1:T(8,128)(4,1)S(1)} %broadcast_compare_fusion.2, bf16[512,16,80]{0,2,1:T(8,128)(2,1)} %bitcast.64, bf16[128,16,80]{0,2,1:T(8,128)(2,1)S(1)} %get-tuple-element.431), kind=kOutput, calls=%fused_computation.2.clone.1 | convolution fusion | flops 170915840 | bytes 5906432 | tf_op jit(solution)/shard_map/while/body/eval_jaxpr/qhd,khd->hqk/dot_general | solution.py:61
  206.9 2.4 copy.43
  209.3 4.8 %fusion.54 = f32[128,16,80]{0,2,1:T(8,128)} fusion(bf16[512,16,80]{0,2,1:T(8,128)(2,1)} %bitcast.65, f32[16,512,128]{2,1,0:T(8,128)} %get-tuple-element.395, f32[16,128]{1,0:T(8,128)S(1)} %get-tuple-element.425, pred[128,512]{0,1:T(8,128)(4,1)S(1)} %broadcast_compare_fusion.2, f32[128,16,80]{0,2,1:T(8,128)} %get-tuple-element.414, ...), kind=kOutput, calls=%fused_computation.8.clone.1 | convolution fusion | flops 173506560 | bytes 6897665 | tf_op jit(solution)/shard_map/while/body/eval_jaxpr/hqk,khd->qhd/dot_general | solution.py:75
  214.2 1.0 fusion.52
  215.3 3.5 %constant_dynamic-slice_fusion.3 = (bf16[512,1280]{1,0:T(8,128)(2,1)}, bf16[512,1280]{1,0:T(8,128)(2,1)}) fusion(bf16[1024,1280]{1,0:T(8,128)(2,1)} %get-tuple-element.432, s32[]{:T(128)S(6)} %select_n.85, bf16[1024,1280]{1,0:T(8,128)(2,1)} %get-tuple-element.430), kind=kLoop, calls=%fused_computation.19.clone.1 | loop fusion | bytes 5242884 | tf_op jit(solution)/shard_map/while/body/eval_jaxpr/dynamic_slice | solution.py:148
  218.7 2.4 copy.42
  221.3 0.1 broadcast_compare_fusion.2
  221.4 4.3 %fusion.50 = (f32[16,128]{1,0:T(8,128)S(1)}, f32[16,512,128]{2,1,0:T(8,128)}) fusion(pred[128,512]{0,1:T(8,128)(4,1)S(1)} %broadcast_compare_fusion.2, bf16[512,16,80]{0,2,1:T(8,128)(2,1)} %bitcast.64, bf16[128,16,80]{0,2,1:T(8,128)(2,1)S(1)} %get-tuple-element.431), kind=kOutput, calls=%fused_computation.2.clone.1 | convolution fusion | flops 170915840 | bytes 5906432 | tf_op jit(solution)/shard_map/while/body/eval_jaxpr/qhd,khd->hqk/dot_general | solution.py:61
  225.7 2.4 copy.43
  228.1 5.0 %fusion.54 = f32[128,16,80]{0,2,1:T(8,128)} fusion(bf16[512,16,80]{0,2,1:T(8,128)(2,1)} %bitcast.65, f32[16,512,128]{2,1,0:T(8,128)} %get-tuple-element.395, f32[16,128]{1,0:T(8,128)S(1)} %get-tuple-element.425, pred[128,512]{0,1:T(8,128)(4,1)S(1)} %broadcast_compare_fusion.2, f32[128,16,80]{0,2,1:T(8,128)} %get-tuple-element.414, ...), kind=kOutput, calls=%fused_computation.8.clone.1 | convolution fusion | flops 173506560 | bytes 6897665 | tf_op jit(solution)/shard_map/while/body/eval_jaxpr/hqk,khd->qhd/dot_general | solution.py:75
  233.1 1.0 fusion.52
  234.2 1.1 divide_convert_fusion
  235.3 45.3 %all-gather.11.cloned.1.call-done = bf16[1280,1280]{1,0:T(8,128)(2,1)} async-done(((bf16[40,1280]{1,0:T(8,128)(2,1)}), bf16[1280,1280]{1,0:T(8,128)(2,1)}) %all-gather.11.cloned.1.call-update) | async-done | bytes 3276816 | tf_op jit(solution)/shard_map/all_gather | solution.py:163
  280.7 3.4 %fusion.18 = bf16[128,1280]{1,0:T(8,128)(2,1)} fusion(f32[128,1280]{1,0:T(8,128)} %copy-done.2, bf16[128,1280]{0,1:T(8,128)(2,1)S(1)} %bitcast.72, bf16[1280,1280]{1,0:T(8,128)(2,1)} %all-gather.11.cloned.1.call-done, f32[1280]{0:T(1024)S(1)} %copy-done.8), kind=kOutput, calls=%fused_computation.27 | convolution fusion | flops 419921920 | bytes 4592640 | tf_op jit(solution)/shard_map/dot_general | solution.py:161
  (47 shorter events, 0.7 us)
Async XLA Ops:
  6.5 29.0 %copy-start = (bf16[1176,1280]{1,0:T(8,128)(2,1)S(1)}, bf16[1176,1280]{1,0:T(8,128)(2,1)}, u32[]{:S(2)}) copy-start(bf16[1176,1280]{1,0:T(8,128)(2,1)} %param.13) | copy-start | bytes 9031684
  6.5 111.7 %all-gather.5.cloned.1.call-start = ((), (), s32[]{:S(2)}) async-start(), calls=%async_computation.1 | async-start | bytes 10137600 | tf_op jit(solution)/shard_map/all_gather | solution.py:109
  9.4 25.0 %all-to-all-start = ((bf16[32,4,1176]{2,1,0:T(4,128)(2,1)}), bf16[32,4,1176]{2,1,0:T(4,128)(2,1)}, u32[]{:S(2)}, u32[]{:S(2)}) async-start(bf16[32,4,1176]{2,1,0:T(4,128)(2,1)} %all_to_all.8), calls=%async_computation | async-start | bytes 655360 | tf_op jit(solution)/shard_map/all_to_all | solution.py:97
  20.8 144.5 %all-gather.7.cloned.1.call-start = ((), (), s32[]{:S(2)}) async-start(), calls=%async_computation.2 | async-start | bytes 2949120 | tf_op jit(solution)/shard_map/all_gather | solution.py:140
  23.7 94.6 %copy-start.4 = (f32[1280]{0:T(1024)S(1)}, f32[1280]{0:T(1024)}, u32[]{:S(2)}) copy-start(f32[1280]{0:T(1024)} %param.15) | copy-start | bytes 15364
  23.7 94.6 %copy-start.5 = (f32[1280]{0:T(1024)S(1)}, f32[1280]{0:T(1024)}, u32[]{:S(2)}) copy-start(f32[1280]{0:T(1024)} %param.14) | copy-start | bytes 15364
  23.7 94.6 %copy-start.7 = (f32[3840]{0:T(1024)S(1)}, f32[3840]{0:T(1024)}, u32[]{:S(2)}) copy-start(f32[3840]{0:T(1024)} %param.17) | copy-start | bytes 46084
  36.2 0.9 copy-start.2
  123.8 1.3 copy-start.3
  137.4 59.1 %copy-start.6 = (s32[1,3]{1,0:T(1,128)S(1)}, s32[1,3]{1,0:T(1,128)}, u32[]{:S(2)}) copy-start(s32[1,3]{1,0:T(1,128)} %param.20) | copy-start | bytes 40
  140.3 56.1 %all-gather.9.cloned.1.call-start = ((), (), s32[]{:S(2)}) async-start(), calls=%async_computation.3 | async-start | bytes 2949120 | tf_op jit(solution)/shard_map/all_gather | solution.py:141
  142.2 138.4 %all-gather.11.cloned.1.call-start = ((), (), s32[]{:S(2)}) async-start(), calls=%async_computation.4 | async-start | bytes 3379200 | tf_op jit(solution)/shard_map/all_gather | solution.py:163
  196.5 84.2 %copy-start.8 = (f32[1280]{0:T(1024)S(1)}, f32[1280]{0:T(1024)}, u32[]{:S(2)}) copy-start(f32[1280]{0:T(1024)} %param.19) | copy-start | bytes 15364
  209.3 4.9 %copy-start.1 = (f32[16,512,128]{2,1,0:T(8,128)S(1)}, f32[16,512,128]{2,1,0:T(8,128)}, u32[]{:S(2)}) copy-start(f32[16,512,128]{2,1,0:T(8,128)} %get-tuple-element.395) | copy-start | bytes 12582916 | tf_op jit(solution)/shard_map/while
  228.1 5.0 %copy-start.1 = (f32[16,512,128]{2,1,0:T(8,128)S(1)}, f32[16,512,128]{2,1,0:T(8,128)}, u32[]{:S(2)}) copy-start(f32[16,512,128]{2,1,0:T(8,128)} %get-tuple-element.395) | copy-start | bytes 12582916 | tf_op jit(solution)/shard_map/while
Sparse Core Ops, SparseCore 0:
  10.0 108.2 all-gather.4
  140.4 24.8 all-gather.6
  167.2 29.2 all-gather.8
  198.9 81.7 all-gather.10
where the time goes:
time: 291 us
  waiting for transfers between devices  188 us (65%)
  local copies, waits for them, and re-layouts  38 us (13%)
  matrix products  28.1 us (10%)
  between operations  13.3 us (5%)
  starting transfers between devices  11.6 us (4%)
  other arithmetic  11.2 us (4%)
    all_gather x1, waiting for transfers between devices, per_device(): lax.all_gather(qkv_weight, 'dp', axis=0, tiled=True)  81 us
    all_gather x1, waiting for transfers between devices, per_device(): lax.all_gather(out_weight, 'dp', axis=0, tiled=True)  45.3 us
    all_gather x1, waiting for transfers between devices, per_device(): piece_values = lax.all_gather(values, 'seq', axis=0, tiled=True)  31.1 us
    all_gather x1, waiting for transfers between devices, per_device(): piece_keys = lax.all_gather(key_rows, 'seq', axis=0, tiled=True)  21.3 us
    dynamic_slice x4, local copies, waits for them, and re-layouts, one_block(): value_block = lax.dynamic_slice_in_dim(piece_values, first_row, length, 0)  11.8 us
    all_to_all x1, starting transfers between devices, per_device(): lax.all_to_all(pixels, 'dp', split_axis=0, concat_axis=0, tiled=True)  11.4 us
    dot_general x2, matrix products, attend_block(): jnp.einsum('hqk,khd->qhd', weights.astype(jnp.bfloat16), value_block.resh...  9.84 us
    dot_general x2, matrix products, attend_block(): jnp.einsum('qhd,khd->hqk', queries3, key_block.reshape(count, HEADS, HDIM...  8.54 us
  transfers between devices with their start and end apart: 5, of which 5 were waited for; matrix products, arithmetic and copies ran while one was open for 17% of the time, Pallas kernels for 0%

commit v1 on v0

--- a/solution.py
+++ b/solution.py
@@ -137,7 +137,12 @@
         jnp.zeros((HEADS, tok_rows), jnp.float32),
         jnp.zeros((tok_rows, HEADS, HDIM), jnp.float32),
     )
-    piece_keys = lax.all_gather(key_rows, "seq", axis=0, tiled=True)
+    ring = [key_rows]
+    for hop in range(7):
+        ring.append(lax.ppermute(ring[-1], "seq", [(dev, (dev + 1) % 8) for dev in range(8)]))
+    piece_keys = jnp.roll(
+        jnp.concatenate(ring[::-1], axis=0), (lax.axis_index("seq") + 1) * ring[0].shape[0], axis=0
+    )
     piece_values = lax.all_gather(values, "seq", axis=0, tiled=True)
     count = piece_keys.shape[0]
     length = block_length(count)

time: 291 us -> 288 us (0.990)
  waiting for transfers between devices: 188 us -> 169 us
  local copies, waits for them, and re-layouts: 38 us -> 53.6 us
    ppermute x0 -> x7, waiting for transfers between devices: none -> 44.6 us  [per_device(): lax.ppermute(ring[-1], 'seq', [(dev, (dev + 1) % 8) for dev in range(8)])]
    all_gather x1, waiting for transfers between devices: 31.1 us -> 0.01 us  [per_device(): piece_values = lax.all_gather(values, 'seq', axis=0, tiled=True)]
    all_gather x1 -> x0, waiting for transfers between devices: 21.3 us -> none  [per_device(): piece_keys = lax.all_gather(key_rows, 'seq', axis=0, tiled=True)]
    all_gather x1, waiting for transfers between devices: 45.3 us -> 31.2 us  [per_device(): lax.all_gather(out_weight, 'dp', axis=0, tiled=True)]
    unnamed x17 -> x56, local copies, waits for them, and re-layouts: 3.46 us -> 17.1 us
    all_to_all x1, waiting for transfers between devices: 8.46 us -> 11.9 us  [per_device(): lax.all_to_all(pixels, 'dp', split_axis=0, concat_axis=0, tiled=True)]
  transfers between devices with their start and end apart: 5 -> 11, of which waited for: 5 -> 10; matrix products, arithmetic and copies ran while one was open for 17% -> 26% of each run, Pallas kernels for 0% -> 0%
where the time goes in v1:
time: 288 us; the launch traced here: 287 us
  waiting for transfers between devices  169 us (59%)
  local copies, waits for them, and re-layouts  53.6 us (19%)
  matrix products  28 us (10%)
  between operations  13.5 us (5%)
  starting transfers between devices  11.6 us (4%)
  other arithmetic  11.2 us (4%)
    all_gather x1, waiting for transfers between devices, per_device(): lax.all_gather(qkv_weight, 'dp', axis=0, tiled=True)  80.9 us
    ppermute x7, waiting for transfers between devices, per_device(): lax.ppermute(ring[-1], 'seq', [(dev, (dev + 1) % 8) for dev in range(8)])  44.6 us
    all_gather x1, waiting for transfers between devices, per_device(): lax.all_gather(out_weight, 'dp', axis=0, tiled=True)  31.2 us
    unnamed x56, local copies, waits for them, and re-layouts  17.1 us
    all_to_all x1, waiting for transfers between devices, per_device(): lax.all_to_all(pixels, 'dp', split_axis=0, concat_axis=0, tiled=True)  11.9 us
    dynamic_slice x4, local copies, waits for them, and re-layouts, one_block(): value_block = lax.dynamic_slice_in_dim(piece_values, first_row, length, 0)  11.8 us
    all_to_all x1, starting transfers between devices, per_device(): lax.all_to_all(pixels, 'dp', split_axis=0, concat_axis=0, tiled=True)  11.4 us
    dot_general x2, matrix products, attend_block(): jnp.einsum('hqk,khd->qhd', weights.astype(jnp.bfloat16), value_block.resh...  9.84 us
  transfers between devices with their start and end apart: 11, of which 10 were waited for; matrix products, arithmetic and copies ran while one was open for 26% of the time, Pallas kernels for 0%

profile of v1, /device:TPU:8, one launch (start us, length us, event | category | flops | bytes accessed | tf_op | source)
XLA Modules:
  0.0 287.2 jit_solution(8920713215559462727)
XLA Ops:
  7.3 1.3 copy.27
  9.4 11.4 %all-to-all-start = ((bf16[32,4,1176]{2,1,0:T(4,128)(2,1)}), bf16[32,4,1176]{2,1,0:T(4,128)(2,1)}, u32[]{:S(2)}, u32[]{:S(2)}) async-start(bf16[32,4,1176]{2,1,0:T(4,128)(2,1)} %all_to_all.8), calls=%async_computation | async-start | bytes 655360 | tf_op jit(solution)/shard_map/all_to_all | solution.py:97
  22.6 11.9 %all-to-all-done = bf16[32,4,1176]{2,1,0:T(4,128)(2,1)} async-done(((bf16[32,4,1176]{2,1,0:T(4,128)(2,1)}), bf16[32,4,1176]{2,1,0:T(4,128)(2,1)}, u32[]{:S(2)}, u32[]{:S(2)}) %all-to-all-start) | async-done | bytes 301088 | tf_op jit(solution)/shard_map/all_to_all | solution.py:97
  34.4 1.1 all_to_all.10
  37.4 80.9 %all-gather.4.cloned.1.call-done = bf16[1280,3840]{1,0:T(8,128)(2,1)} async-done(((bf16[40,3840]{1,0:T(8,128)(2,1)}), bf16[1280,3840]{1,0:T(8,128)(2,1)}) %all-gather.4.cloned.1.call-update) | async-done | bytes 9830416 | tf_op jit(solution)/shard_map/all_gather | solution.py:109
  118.2 5.5 %convolution_add_fusion = f32[128,3840]{1,0:T(8,128)S(1)} fusion(bf16[1280,3840]{1,0:T(8,128)(2,1)} %all-gather.4.cloned.1.call-done, f32[3840]{0:T(1024)S(1)} %copy-done.19, f32[128,1280]{1,0:T(8,128)} %copy-done.2, f32[1280]{0:T(1024)S(1)} %copy-done.16, f32[1280]{0:T(1024)S(1)} %copy-done.17, f32[128]{0:T(128)S(1)} %add_rsqrt_fusion, ...), kind=kOutput, calls=%fused_computation.24 | convolution fusion | flops 1259601920 | bytes 12478464 | tf_op jit(solution)/shard_map/dot_general | solution.py:107
  123.8 1.3 copy-done.3
  127.1 2.2 copy.28
  129.2 2.4 fusion.27
  131.7 2.2 copy.29
  133.9 2.2 copy.32
  136.1 1.4 slice_negate_fusion
  137.4 1.2 maximum_multiply_fusion.1
  138.6 2.2 copy.30
  140.8 2.2 copy.33
  143.0 2.8 add_convert_fusion
  146.5 6.5 %collective-permute-done = bf16[128,1280]{1,0:T(8,128)(2,1)S(1)} collective-permute-done((bf16[128,1280]{1,0:T(8,128)(2,1)S(1)}, bf16[128,1280]{1,0:T(8,128)(2,1)S(1)}, u32[]{:S(2)}, u32[]{:S(2)}) %collective-permute-start) | collective-permute-done | bytes 327712 | tf_op jit(solution)/shard_map/ppermute | solution.py:142
  153.7 6.5 %collective-permute-done.1 = bf16[128,1280]{1,0:T(8,128)(2,1)S(1)} collective-permute-done((bf16[128,1280]{1,0:T(8,128)(2,1)S(1)}, bf16[128,1280]{1,0:T(8,128)(2,1)S(1)}, u32[]{:S(2)}, u32[]{:S(2)}) %collective-permute-start.1) | collective-permute-done | bytes 327712 | tf_op jit(solution)/shard_map/ppermute | solution.py:142
  161.0 6.5 %collective-permute-done.2 = bf16[128,1280]{1,0:T(8,128)(2,1)S(1)} collective-permute-done((bf16[128,1280]{1,0:T(8,128)(2,1)S(1)}, bf16[128,1280]{1,0:T(8,128)(2,1)S(1)}, u32[]{:S(2)}, u32[]{:S(2)}) %collective-permute-start.2) | collective-permute-done | bytes 327712 | tf_op jit(solution)/shard_map/ppermute | solution.py:142
  168.2 6.5 %collective-permute-done.3 = bf16[128,1280]{1,0:T(8,128)(2,1)S(1)} collective-permute-done((bf16[128,1280]{1,0:T(8,128)(2,1)S(1)}, bf16[128,1280]{1,0:T(8,128)(2,1)S(1)}, u32[]{:S(2)}, u32[]{:S(2)}) %collective-permute-start.3) | collective-permute-done | bytes 327712 | tf_op jit(solution)/shard_map/ppermute | solution.py:142
  175.4 6.5 %collective-permute-done.4 = bf16[128,1280]{1,0:T(8,128)(2,1)S(1)} collective-permute-done((bf16[128,1280]{1,0:T(8,128)(2,1)S(1)}, bf16[128,1280]{1,0:T(8,128)(2,1)S(1)}, u32[]{:S(2)}, u32[]{:S(2)}) %collective-permute-start.4) | collective-permute-done | bytes 327712 | tf_op jit(solution)/shard_map/ppermute | solution.py:142
  182.7 6.6 %collective-permute-done.5 = bf16[128,1280]{1,0:T(8,128)(2,1)} collective-permute-done((bf16[128,1280]{1,0:T(8,128)(2,1)S(1)}, bf16[128,1280]{1,0:T(8,128)(2,1)}, u32[]{:S(2)}, u32[]{:S(2)}) %collective-permute-start.5) | collective-permute-done | bytes 327712 | tf_op jit(solution)/shard_map/ppermute | solution.py:142
  189.4 1.2 copy.34
  190.6 5.5 %collective-permute-done.6 = bf16[128,1280]{1,0:T(8,128)(2,1)} collective-permute-done((bf16[128,1280]{1,0:T(8,128)(2,1)}, bf16[128,1280]{1,0:T(8,128)(2,1)}, u32[]{:S(2)}, u32[]{:S(2)}) %collective-permute-start.6) | collective-permute-done | bytes 327712 | tf_op jit(solution)/shard_map/ppermute | solution.py:142
  197.1 1.0 constant_dynamic-update-slice_fusion.14
  198.1 1.0 constant_dynamic-update-slice_fusion.13
  199.1 1.0 constant_dynamic-update-slice_fusion.12
  200.1 1.0 constant_dynamic-update-slice_fusion.11
  201.1 1.0 constant_dynamic-update-slice_fusion.10
  202.1 1.0 constant_dynamic-update-slice_fusion.9
  204.2 1.0 constant_dynamic-update-slice_fusion.6
  205.4 1.7 constant_dynamic-slice_fusion.2
  207.1 37.7 %while.20 = (s32[]{:T(128)}, f32[16,128]{1,0:T(8,128)S(1)}, f32[16,128]{1,0:T(8,128)S(1)}, f32[128,16,80]{0,2,1:T(8,128)}, s32[128]{0:T(128)S(1)}, /*index=5*/s3...) while((s32[]{:T(128)}, f32[16,128]{1,0:T(8,128)S(1)}, ...), condition=%wide.region_9.10_spmd.clone, body=%wide.region_5.9_spmd.clone.sunk | while | flops 349750272 | bytes 44511972 | solution.py:159
  207.1 3.4 %constant_dynamic-slice_fusion.4 = (bf16[512,1280]{1,0:T(8,128)(2,1)}, bf16[512,1280]{1,0:T(8,128)(2,1)}) fusion(bf16[1024,1280]{1,0:T(8,128)(2,1)} %get-tuple-element.432, s32[]{:T(128)S(6)} %select_n.100, bf16[1024,1280]{1,0:T(8,128)(2,1)} %get-tuple-element.430), kind=kLoop, calls=%fused_computation.19.clone.1 | loop fusion | bytes 5242884 | tf_op jit(solution)/shard_map/while/body/eval_jaxpr/dynamic_slice | solution.py:153
  210.6 2.5 copy.42
  213.3 4.3 %fusion.50 = (f32[16,128]{1,0:T(8,128)S(1)}, f32[16,512,128]{2,1,0:T(8,128)}) fusion(pred[128,512]{0,1:T(8,128)(4,1)S(1)} %broadcast_compare_fusion.2, bf16[512,16,80]{0,2,1:T(8,128)(2,1)} %bitcast.64, bf16[128,16,80]{0,2,1:T(8,128)(2,1)S(1)} %get-tuple-element.431), kind=kOutput, calls=%fused_computation.2.clone.1 | convolution fusion | flops 170915840 | bytes 5906432 | tf_op jit(solution)/shard_map/while/body/eval_jaxpr/qhd,khd->hqk/dot_general | solution.py:61
  217.6 2.5 copy.43
  220.0 4.9 %fusion.54 = f32[128,16,80]{0,2,1:T(8,128)} fusion(bf16[512,16,80]{0,2,1:T(8,128)(2,1)} %bitcast.65, f32[16,512,128]{2,1,0:T(8,128)} %get-tuple-element.395, f32[16,128]{1,0:T(8,128)S(1)} %get-tuple-element.425, pred[128,512]{0,1:T(8,128)(4,1)S(1)} %broadcast_compare_fusion.2, f32[128,16,80]{0,2,1:T(8,128)} %get-tuple-element.414, ...), kind=kOutput, calls=%fused_computation.8.clone.1 | convolution fusion | flops 173506560 | bytes 6897665 | tf_op jit(solution)/shard_map/while/body/eval_jaxpr/hqk,khd->qhd/dot_general | solution.py:75
  224.9 1.0 fusion.52
  226.0 3.4 %constant_dynamic-slice_fusion.4 = (bf16[512,1280]{1,0:T(8,128)(2,1)}, bf16[512,1280]{1,0:T(8,128)(2,1)}) fusion(bf16[1024,1280]{1,0:T(8,128)(2,1)} %get-tuple-element.432, s32[]{:T(128)S(6)} %select_n.100, bf16[1024,1280]{1,0:T(8,128)(2,1)} %get-tuple-element.430), kind=kLoop, calls=%fused_computation.19.clone.1 | loop fusion | bytes 5242884 | tf_op jit(solution)/shard_map/while/body/eval_jaxpr/dynamic_slice | solution.py:153
  229.4 2.5 copy.42
  232.1 4.3 %fusion.50 = (f32[16,128]{1,0:T(8,128)S(1)}, f32[16,512,128]{2,1,0:T(8,128)}) fusion(pred[128,512]{0,1:T(8,128)(4,1)S(1)} %broadcast_compare_fusion.2, bf16[512,16,80]{0,2,1:T(8,128)(2,1)} %bitcast.64, bf16[128,16,80]{0,2,1:T(8,128)(2,1)S(1)} %get-tuple-element.431), kind=kOutput, calls=%fused_computation.2.clone.1 | convolution fusion | flops 170915840 | bytes 5906432 | tf_op jit(solution)/shard_map/while/body/eval_jaxpr/qhd,khd->hqk/dot_general | solution.py:61
  236.4 2.5 copy.43
  238.8 5.0 %fusion.54 = f32[128,16,80]{0,2,1:T(8,128)} fusion(bf16[512,16,80]{0,2,1:T(8,128)(2,1)} %bitcast.65, f32[16,512,128]{2,1,0:T(8,128)} %get-tuple-element.395, f32[16,128]{1,0:T(8,128)S(1)} %get-tuple-element.425, pred[128,512]{0,1:T(8,128)(4,1)S(1)} %broadcast_compare_fusion.2, f32[128,16,80]{0,2,1:T(8,128)} %get-tuple-element.414, ...), kind=kOutput, calls=%fused_computation.8.clone.1 | convolution fusion | flops 173506560 | bytes 6897665 | tf_op jit(solution)/shard_map/while/body/eval_jaxpr/hqk,khd->qhd/dot_general | solution.py:75
  243.8 1.0 fusion.52
  244.9 1.1 divide_convert_fusion
  246.0 31.2 %all-gather.8.cloned.1.call-done = bf16[1280,1280]{1,0:T(8,128)(2,1)} async-done(((bf16[40,1280]{1,0:T(8,128)(2,1)}), bf16[1280,1280]{1,0:T(8,128)(2,1)}) %all-gather.8.cloned.1.call-update) | async-done | bytes 3276816 | tf_op jit(solution)/shard_map/all_gather | solution.py:168
  277.2 3.4 %fusion.18 = bf16[128,1280]{1,0:T(8,128)(2,1)} fusion(f32[128,1280]{1,0:T(8,128)} %copy-done.2, bf16[128,1280]{0,1:T(8,128)(2,1)S(1)} %bitcast.72, bf16[1280,1280]{1,0:T(8,128)(2,1)} %all-gather.8.cloned.1.call-done, f32[1280]{0:T(1024)S(1)} %copy-done.20), kind=kOutput, calls=%fused_computation.27 | convolution fusion | flops 419921920 | bytes 4592640 | tf_op jit(solution)/shard_map/dot_general | solution.py:166
  (99 shorter events, 14.1 us)
Async XLA Ops:
  6.5 29.0 %copy-start = (bf16[1176,1280]{1,0:T(8,128)(2,1)S(1)}, bf16[1176,1280]{1,0:T(8,128)(2,1)}, u32[]{:S(2)}) copy-start(bf16[1176,1280]{1,0:T(8,128)(2,1)} %param.13) | copy-start | bytes 9031684
  6.5 111.7 %copy-start.17 = (f32[1280]{0:T(1024)S(1)}, f32[1280]{0:T(1024)}, u32[]{:S(2)}) copy-start(f32[1280]{0:T(1024)} %param.14) | copy-start | bytes 15364
  6.5 111.7 %copy-start.16 = (f32[1280]{0:T(1024)S(1)}, f32[1280]{0:T(1024)}, u32[]{:S(2)}) copy-start(f32[1280]{0:T(1024)} %param.15) | copy-start | bytes 15364
  6.5 111.7 %copy-start.19 = (f32[3840]{0:T(1024)S(1)}, f32[3840]{0:T(1024)}, u32[]{:S(2)}) copy-start(f32[3840]{0:T(1024)} %param.17) | copy-start | bytes 46084
  6.5 111.7 %all-gather.4.cloned.1.call-start = ((), (), s32[]{:S(2)}) async-start(), calls=%async_computation.1 | async-start | bytes 10137600 | tf_op jit(solution)/shard_map/all_gather | solution.py:109
  9.4 25.0 %all-to-all-start = ((bf16[32,4,1176]{2,1,0:T(4,128)(2,1)}), bf16[32,4,1176]{2,1,0:T(4,128)(2,1)}, u32[]{:S(2)}, u32[]{:S(2)}) async-start(bf16[32,4,1176]{2,1,0:T(4,128)(2,1)} %all_to_all.8), calls=%async_computation | async-start | bytes 655360 | tf_op jit(solution)/shard_map/all_to_all | solution.py:97
  20.9 186.3 %all-gather.6.cloned.1.call-start = ((), (), s32[]{:S(2)}) async-start(), calls=%async_computation.2 | async-start | bytes 2949120 | tf_op jit(solution)/shard_map/all_gather | solution.py:146
  36.3 0.9 copy-start.2
  123.8 1.3 copy-start.3
  125.9 151.4 %all-gather.8.cloned.1.call-start = ((), (), s32[]{:S(2)}) async-start(), calls=%async_computation.3 | async-start | bytes 3379200 | tf_op jit(solution)/shard_map/all_gather | solution.py:168
  145.8 0.7 copy-start.4
  146.5 6.5 %collective-permute-start = (bf16[128,1280]{1,0:T(8,128)(2,1)S(1)}, bf16[128,1280]{1,0:T(8,128)(2,1)S(1)}, u32[]{:S(2)}, u32[]{:S(2)}) collective-permute-start(bf16[128,1280]{1,0:T(8,128)(2,1)S(1)} %get-tuple-element.314), channel_id=1, source_target_pairs={{0,1},{1,2},{2,3},{3,4},{4,5},{5,6},{6,7},{7,0},{8,9},{9,10},{10,1... | collective-permute-start | bytes 983048 | tf_op jit(solution)/shard_map/ppermute | solution.py:142
  153.0 0.7 copy-start.6
  153.7 6.5 %collective-permute-start.1 = (bf16[128,1280]{1,0:T(8,128)(2,1)S(1)}, bf16[128,1280]{1,0:T(8,128)(2,1)S(1)}, u32[]{:S(2)}, u32[]{:S(2)}) collective-permute-start(bf16[128,1280]{1,0:T(8,128)(2,1)S(1)} %collective-permute-done), channel_id=1, source_target_pairs={{0,1},{1,2},{2,3},{3,4},{4,5},{5,6},{6,7},{7,0},{8,9},{9,10},{10,1... | collective-permute-start | bytes 983048 | tf_op jit(solution)/shard_map/ppermute | solution.py:142
  160.2 0.8 copy-start.8
  161.0 6.5 %collective-permute-start.2 = (bf16[128,1280]{1,0:T(8,128)(2,1)S(1)}, bf16[128,1280]{1,0:T(8,128)(2,1)S(1)}, u32[]{:S(2)}, u32[]{:S(2)}) collective-permute-start(bf16[128,1280]{1,0:T(8,128)(2,1)S(1)} %collective-permute-done.1), channel_id=1, source_target_pairs={{0,1},{1,2},{2,3},{3,4},{4,5},{5,6},{6,7},{7,0},{8,9},{9,10},{10,1... | collective-permute-start | bytes 983048 | tf_op jit(solution)/shard_map/ppermute | solution.py:142
  167.5 0.7 copy-start.10
  168.2 6.5 %collective-permute-start.3 = (bf16[128,1280]{1,0:T(8,128)(2,1)S(1)}, bf16[128,1280]{1,0:T(8,128)(2,1)S(1)}, u32[]{:S(2)}, u32[]{:S(2)}) collective-permute-start(bf16[128,1280]{1,0:T(8,128)(2,1)S(1)} %collective-permute-done.2), channel_id=1, source_target_pairs={{0,1},{1,2},{2,3},{3,4},{4,5},{5,6},{6,7},{7,0},{8,9},{9,10},{10,1... | collective-permute-start | bytes 983048 | tf_op jit(solution)/shard_map/ppermute | solution.py:142
  174.7 0.7 copy-start.12
  175.4 6.5 %collective-permute-start.4 = (bf16[128,1280]{1,0:T(8,128)(2,1)S(1)}, bf16[128,1280]{1,0:T(8,128)(2,1)S(1)}, u32[]{:S(2)}, u32[]{:S(2)}) collective-permute-start(bf16[128,1280]{1,0:T(8,128)(2,1)S(1)} %collective-permute-done.3), channel_id=1, source_target_pairs={{0,1},{1,2},{2,3},{3,4},{4,5},{5,6},{6,7},{7,0},{8,9},{9,10},{10,1... | collective-permute-start | bytes 983048 | tf_op jit(solution)/shard_map/ppermute | solution.py:142
  181.9 0.7 copy-start.14
  182.7 6.6 %collective-permute-start.5 = (bf16[128,1280]{1,0:T(8,128)(2,1)S(1)}, bf16[128,1280]{1,0:T(8,128)(2,1)}, u32[]{:S(2)}, u32[]{:S(2)}) collective-permute-start(bf16[128,1280]{1,0:T(8,128)(2,1)S(1)} %collective-permute-done.4), channel_id=1, source_target_pairs={{0,1},{1,2},{2,3},{3,4},{4,5},{5,6},{6,7},{7,0},{8,9},{9,10},{10,1... | collective-permute-start | bytes 983048 | tf_op jit(solution)/shard_map/ppermute | solution.py:142
  189.3 6.8 %collective-permute-start.6 = (bf16[128,1280]{1,0:T(8,128)(2,1)}, bf16[128,1280]{1,0:T(8,128)(2,1)}, u32[]{:S(2)}, u32[]{:S(2)}) collective-permute-start(bf16[128,1280]{1,0:T(8,128)(2,1)} %collective-permute-done.5), channel_id=1, source_target_pairs={{0,1},{1,2},{2,3},{3,4},{4,5},{5,6},{6,7},{7,0},{8,9},{9,10},{10,1... | collective-permute-start | bytes 983048 | tf_op jit(solution)/shard_map/ppermute | solution.py:142
  190.5 12.6 %copy-start.5 = (bf16[128,1280]{1,0:T(8,128)(2,1)S(1)}, bf16[128,1280]{1,0:T(8,128)(2,1)}, u32[]{:S(2)}) copy-start(bf16[128,1280]{1,0:T(8,128)(2,1)} %copy-done.4) | copy-start | bytes 983044
  190.5 14.6 %copy-start.15 = (bf16[128,1280]{1,0:T(8,128)(2,1)S(1)}, bf16[128,1280]{1,0:T(8,128)(2,1)}, u32[]{:S(2)}) copy-start(bf16[128,1280]{1,0:T(8,128)(2,1)} %copy-done.14) | copy-start | bytes 983044
  190.6 14.7 %copy-start.13 = (bf16[128,1280]{1,0:T(8,128)(2,1)S(1)}, bf16[128,1280]{1,0:T(8,128)(2,1)}, u32[]{:S(2)}) copy-start(bf16[128,1280]{1,0:T(8,128)(2,1)} %copy-done.12) | copy-start | bytes 983044
  190.6 14.7 %copy-start.11 = (bf16[128,1280]{1,0:T(8,128)(2,1)S(1)}, bf16[128,1280]{1,0:T(8,128)(2,1)}, u32[]{:S(2)}) copy-start(bf16[128,1280]{1,0:T(8,128)(2,1)} %copy-done.10) | copy-start | bytes 983044
  190.6 14.7 %copy-start.9 = (bf16[128,1280]{1,0:T(8,128)(2,1)S(1)}, bf16[128,1280]{1,0:T(8,128)(2,1)}, u32[]{:S(2)}) copy-start(bf16[128,1280]{1,0:T(8,128)(2,1)} %copy-done.8) | copy-start | bytes 983044
  197.1 8.3 %copy-start.7 = (bf16[128,1280]{1,0:T(8,128)(2,1)S(1)}, bf16[128,1280]{1,0:T(8,128)(2,1)}, u32[]{:S(2)}) copy-start(bf16[128,1280]{1,0:T(8,128)(2,1)} %copy-done.6) | copy-start | bytes 983044
  205.2 1.9 copy-start.18
  207.1 70.1 %copy-start.20 = (f32[1280]{0:T(1024)S(1)}, f32[1280]{0:T(1024)}, u32[]{:S(2)}) copy-start(f32[1280]{0:T(1024)} %param.19) | copy-start | bytes 15364
  220.0 4.9 %copy-start.1 = (f32[16,512,128]{2,1,0:T(8,128)S(1)}, f32[16,512,128]{2,1,0:T(8,128)}, u32[]{:S(2)}) copy-start(f32[16,512,128]{2,1,0:T(8,128)} %get-tuple-element.395) | copy-start | bytes 12582916 | tf_op jit(solution)/shard_map/while
  238.8 5.0 %copy-start.1 = (f32[16,512,128]{2,1,0:T(8,128)S(1)}, f32[16,512,128]{2,1,0:T(8,128)}, u32[]{:S(2)}) copy-start(f32[16,512,128]{2,1,0:T(8,128)} %get-tuple-element.395) | copy-start | bytes 12582916 | tf_op jit(solution)/shard_map/while
Sparse Core Ops, SparseCore 0:
  10.0 108.2 all-gather.3
  126.0 24.8 all-gather.5
  189.4 87.7 all-gather.7
